TPU v7x, 32 devices: a whole 2x2x4 slice. The times are simulated.
32 devices in a mesh: leaf: 8 (over z, x), row: 4 (over y, core).
Axes of the slice: x: 2, y: 2, z: 4, core: 2. Of those that a mesh axis runs over, the one named last changes fastest.
Arguments:
- sec_rhs: float32 [64, 4096], P(None, ('leaf', 'row')), may hold values from -6 to 6
- sec_inverse: float32 [4096, 512], P(('leaf', 'row')), as said below
- sep_rhs: float32 [4, 64, 1024], P(None, None, 'leaf'), may hold values from -6 to 6
- sep_inverse: float32 [4, 1024, 1024], P(None, 'leaf'), as said below
- sep_coupling: float32 [3, 1024, 1024], P(None, 'leaf'), may hold values from -0.1875 to 0.1875
- sec_update: float32 [4, 1024, 4096], P(None, None, ('leaf', 'row')), may hold values from -0.1875 to 0.1875
- link: int32 [8, 4], P('leaf'), may hold values 0 or 1
Outputs:
- sec_solution: float32 [64, 4096], P(None, ('leaf', 'row'))
- sep_solution: float32 [4, 64, 1024], P(None, None, 'leaf')
Inputs may be any that keep to these rules, and one draw needn't show every extreme that they name: link holds only 0 and 1. Each section's block of sec_inverse is lower triangular with entries on the diagonal between 0.7 and 1.3. Each block of sep_inverse is lower triangular with entries on the diagonal between 0.7 and 1.3.
All inputs are finite; a program needn't handle non-finite values. No bound on the sum of `link` on one device may be relied on, other than what follows from the above.
Results may differ from a plain program's by a relative error of at most 0.00013.
Values sent between devices are 32-bit elements; how exact they have to be, the bound alone decides.
A program may use at most 128 MiB of HBM per device.

v0:
```python
import jax
import jax.numpy as jnp
from jax import lax
from jax.sharding import PartitionSpec as P


def dot_last(left, right):
    return lax.dot_general(
        left,
        right,
        (((1,), (1,)), ((), ())),
        precision=lax.Precision.HIGHEST,
        preferred_element_type=jnp.float32,
    )


def dot_plain(left, right):
    return jnp.dot(left, right, precision=lax.Precision.HIGHEST, preferred_element_type=jnp.float32)


def per_device(sec_rhs, sec_inverse, sep_rhs, sep_inverse, sep_coupling, sec_update, link):
    highest = lax.Precision.HIGHEST
    levels = sep_rhs.shape[0]
    link_weights = link[0].astype(jnp.float32)
    rhs_full = lax.all_gather(sec_rhs, "row", axis=1, tiled=True)
    y_sec = dot_last(rhs_full, sec_inverse)
    section_parts = (
        jnp.einsum("rj,kmj->krm", y_sec, sec_update, precision=highest)
        * link_weights[:, None, None]
    )
    row_total = lax.psum(section_parts, "row")
    reduced = lax.psum_scatter(row_total, "leaf", scatter_dimension=2, tiled=True)
    y_leaf = []
    y_full = None
    for level in range(levels):
        known_part = sep_rhs[level] - reduced[level]
        if level > 0:
            known_part = known_part - dot_last(y_full, sep_coupling[level - 1])
        known_full = lax.all_gather(known_part, "leaf", axis=1, tiled=True)
        y_level = dot_last(known_full, sep_inverse[level])
        y_leaf.append(y_level)
        if level < levels - 1:
            y_full = lax.all_gather(y_level, "leaf", axis=1, tiled=True)
    solved = [None] * levels
    rhs_width = y_leaf[0].shape[0] // lax.axis_size("row")
    rhs_start = lax.axis_index("row") * rhs_width
    for level in range(levels - 1, -1, -1):
        adjusted = lax.dynamic_slice_in_dim(y_leaf[level], rhs_start, rhs_width, 0)
        if level < levels - 1:
            coupling_part = dot_plain(solved[level + 1], sep_coupling[level])
            adjusted = adjusted - lax.psum_scatter(
                coupling_part, "leaf", scatter_dimension=1, tiled=True
            )
        solve_part = dot_plain(adjusted, sep_inverse[level])
        solved[level] = lax.psum_scatter(solve_part, "leaf", scatter_dimension=1, tiled=True)
    solved_stack = lax.all_gather(jnp.stack(solved), "row", axis=1, tiled=True)
    solved_full = lax.all_gather(solved_stack, "leaf", axis=2, tiled=True)
    weighted = solved_full * link_weights[:, None, None]
    back_sec = y_sec - jnp.einsum("krm,kmj->rj", weighted, sec_update, precision=highest)
    section_part = dot_plain(back_sec, sec_inverse)
    sec_solution = lax.psum_scatter(section_part, "row", scatter_dimension=1, tiled=True)
    return (sec_solution, solved_stack)


def solution(mesh):
    in_specs = (
        P(None, ("leaf", "row")),
        P(("leaf", "row"), None),
        P(None, None, "leaf"),
        P(None, "leaf", None),
        P(None, "leaf", None),
        P(None, None, ("leaf", "row")),
        P("leaf", None),
    )
    out_specs = (P(None, ("leaf", "row")), P(None, None, "leaf"))
    return jax.shard_map(
        per_device, mesh=mesh, in_specs=in_specs, out_specs=out_specs, check_vma=False
    )
```

profile of v0, /device:TPU:0, one launch (start us, length us, event | category | flops | bytes accessed | tf_op | source)
XLA Modules:
  0.0 811.1 jit_solution(3679977903072324729)
XLA Ops:
  7.2 6.9 all_gather.30
  14.1 0.7 convert_bitcast_fusion
  14.7 1.3 fusion.59
  16.1 3.3 fusion
  19.5 65.5 %reduce-scatter.26.cloned.1.call-done = f32[4,64,128]{2,1,0:T(8,128)} async-done(((f32[4,64,1024]{2,1,0:T(8,128)}), f32[4,64,128]{2,1,0:T(8,128)}) %reduce-scatter.26.cloned.1.call-update) | async-done | bytes 131088 | tf_op jit(solution)/shard_map/reduce_scatter | solution.py:32
  85.1 32.8 %all-reduce.2.cloned.1.call-done = f32[4,64,128]{2,1,0:T(8,128)} async-done(((f32[4,64,128]{2,1,0:T(8,128)}), f32[4,64,128]{2,1,0:T(8,128)}) %all-reduce.2.cloned.1.call-update) | async-done | bytes 131088 | tf_op jit(solution)/shard_map/psum | solution.py:31
  118.0 0.9 slice_subtract_fusion.3
  118.9 31.0 %all-gather = f32[1,64,1024]{2,1,0:T(8,128)S(1)} all-gather(f32[1,64,128]{2,1,0:T(8,128)S(1)} %slice_subtract_fusion.3), channel_id=2, replica_groups=mesh['leaf'=8,'row'=4] {'leaf'}, dimensions={2}, use_global_device_ids=true | all-gather | bytes 294912 | tf_op jit(solution)/shard_map/all_gather | solution.py:39
  149.9 1.7 fusion.26
  151.6 30.8 %all_gather.32 = f32[64,1024]{1,0:T(8,128)S(1)} all-gather(f32[64,128]{1,0:T(8,128)S(1)} %fusion.26), channel_id=1, replica_groups=mesh['leaf'=8,'row'=4] {'leaf'}, dimensions={1}, use_global_device_ids=true | all-gather | bytes 294912 | tf_op jit(solution)/shard_map/all_gather | solution.py:43
  182.4 1.7 convolution_subtract_fusion.2
  184.1 31.0 %all_gather.33 = f32[64,1024]{1,0:T(8,128)S(1)} all-gather(f32[64,128]{1,0:T(8,128)S(1)} %convolution_subtract_fusion.2), channel_id=1, replica_groups=mesh['leaf'=8,'row'=4] {'leaf'}, dimensions={1}, use_global_device_ids=true | all-gather | bytes 294912 | tf_op jit(solution)/shard_map/all_gather | solution.py:39
  215.1 0.7 fusion.19
  215.8 30.8 %all_gather.34 = f32[64,1024]{1,0:T(8,128)S(1)} all-gather(f32[64,128]{1,0:T(8,128)S(1)} %fusion.19), channel_id=1, replica_groups=mesh['leaf'=8,'row'=4] {'leaf'}, dimensions={1}, use_global_device_ids=true | all-gather | bytes 294912 | tf_op jit(solution)/shard_map/all_gather | solution.py:43
  246.5 1.4 convolution_subtract_fusion.1
  248.0 30.7 %all_gather.35 = f32[64,1024]{1,0:T(8,128)S(1)} all-gather(f32[64,128]{1,0:T(8,128)S(1)} %convolution_subtract_fusion.1), channel_id=1, replica_groups=mesh['leaf'=8,'row'=4] {'leaf'}, dimensions={1}, use_global_device_ids=true | all-gather | bytes 294912 | tf_op jit(solution)/shard_map/all_gather | solution.py:39
  278.7 0.7 fusion.12
  279.4 30.7 %all_gather.36 = f32[64,1024]{1,0:T(8,128)S(1)} all-gather(f32[64,128]{1,0:T(8,128)S(1)} %fusion.12), channel_id=1, replica_groups=mesh['leaf'=8,'row'=4] {'leaf'}, dimensions={1}, use_global_device_ids=true | all-gather | bytes 294912 | tf_op jit(solution)/shard_map/all_gather | solution.py:43
  310.1 1.4 convolution_subtract_fusion
  311.5 30.7 %all_gather.37 = f32[64,1024]{1,0:T(8,128)S(1)} all-gather(f32[64,128]{1,0:T(8,128)S(1)} %convolution_subtract_fusion), channel_id=1, replica_groups=mesh['leaf'=8,'row'=4] {'leaf'}, dimensions={1}, use_global_device_ids=true | all-gather | bytes 294912 | tf_op jit(solution)/shard_map/all_gather | solution.py:39
  342.3 0.7 fusion.5
  342.9 1.0 fusion.3
  344.0 53.8 %reduce-scatter.10.cloned.1.call-done = f32[16,128]{1,0:T(8,128)} async-done(((f32[16,1024]{1,0:T(8,128)}), f32[16,128]{1,0:T(8,128)}) %reduce-scatter.10.cloned.1.call-update) | async-done | bytes 8208 | tf_op jit(solution)/shard_map/reduce_scatter | solution.py:55
  397.8 2.1 fusion.7
  399.9 54.2 %reduce-scatter.12.cloned.1.call-done = f32[16,128]{1,0:T(8,128)} async-done(((f32[16,1024]{1,0:T(8,128)}), f32[16,128]{1,0:T(8,128)}) %reduce-scatter.12.cloned.1.call-update) | async-done | bytes 8208 | tf_op jit(solution)/shard_map/reduce_scatter | solution.py:51
  454.1 2.1 fusion.10
  456.2 0.0 reduce-scatter.16.cloned.1.call-start
  456.2 54.2 %reduce-scatter.14.cloned.1.call-done = f32[16,128]{1,0:T(8,128)} async-done(((f32[16,1024]{1,0:T(8,128)}), f32[16,128]{1,0:T(8,128)}) %reduce-scatter.14.cloned.1.call-update) | async-done | bytes 8208 | tf_op jit(solution)/shard_map/reduce_scatter | solution.py:55
  510.4 2.1 fusion.14
  512.5 0.0 reduce-scatter.18.cloned.1.call-start
  512.6 54.2 %reduce-scatter.16.cloned.1.call-done = f32[16,128]{1,0:T(8,128)} async-done(((f32[16,1024]{1,0:T(8,128)}), f32[16,128]{1,0:T(8,128)}) %reduce-scatter.16.cloned.1.call-update) | async-done | bytes 8208 | tf_op jit(solution)/shard_map/reduce_scatter | solution.py:51
  566.7 2.1 fusion.17
  568.8 0.0 reduce-scatter.20.cloned.1.call-start
  568.9 54.3 %reduce-scatter.18.cloned.1.call-done = f32[16,128]{1,0:T(8,128)} async-done(((f32[16,1024]{1,0:T(8,128)}), f32[16,128]{1,0:T(8,128)}) %reduce-scatter.18.cloned.1.call-update) | async-done | bytes 8208 | tf_op jit(solution)/shard_map/reduce_scatter | solution.py:55
  623.2 2.1 fusion.21
  625.3 0.0 reduce-scatter.22.cloned.1.call-start
  625.3 54.3 %reduce-scatter.20.cloned.1.call-done = f32[16,128]{1,0:T(8,128)} async-done(((f32[16,1024]{1,0:T(8,128)}), f32[16,128]{1,0:T(8,128)}) %reduce-scatter.20.cloned.1.call-update) | async-done | bytes 8208 | tf_op jit(solution)/shard_map/reduce_scatter | solution.py:51
  679.7 2.1 fusion.24
  681.7 0.0 all-gather.3.cloned.1.call-start
  681.8 54.4 %reduce-scatter.22.cloned.1.call-done = f32[16,128]{1,0:T(8,128)} async-done(((f32[16,1024]{1,0:T(8,128)}), f32[16,128]{1,0:T(8,128)}) %reduce-scatter.22.cloned.1.call-update) | async-done | bytes 8208 | tf_op jit(solution)/shard_map/reduce_scatter | solution.py:55
  736.2 0.7 pad_maximum_fusion
  736.9 5.9 all_gather.38
  742.8 0.0 reduce-scatter.24.cloned.1.call-start
  742.9 38.7 %all-gather.3.cloned.1.call-done = f32[4,64,1024]{2,1,0:T(8,128)} async-done(((f32[4,64,128]{2,1,0:T(8,128)}), f32[4,64,1024]{2,1,0:T(8,128)}) %all-gather.3.cloned.1.call-update) | async-done | bytes 1048592 | tf_op jit(solution)/shard_map/all_gather | solution.py:57
  781.6 2.7 fusion.1
  784.3 0.9 fusion.60
  785.2 18.6 %reduce-scatter.24.cloned.1.call-done = f32[64,128]{1,0:T(8,128)} async-done(((f32[64,512]{1,0:T(8,128)}), f32[64,128]{1,0:T(8,128)}) %reduce-scatter.24.cloned.1.call-update) | async-done | bytes 32784 | tf_op jit(solution)/shard_map/reduce_scatter | solution.py:61
  803.9 0.7 copy.11
  (32 shorter events, 0.4 us)
Async XLA Ops:
  7.2 8.9 %copy-start = (f32[4,1024,128]{2,1,0:T(8,128)S(1)}, f32[4,1024,128]{2,1,0:T(8,128)}, u32[]{:S(2)}) copy-start(f32[4,1024,128]{2,1,0:T(8,128)} %param.12) | copy-start | bytes 6291460
  7.2 77.9 %reduce-scatter.26.cloned.1.call-start = ((), (), s32[]{:S(2)}) async-start(), calls=%async_computation.18 | async-start | bytes 1179648 | tf_op jit(solution)/shard_map/reduce_scatter | solution.py:32
  16.1 101.9 %copy-start.5 = (f32[4,64,128]{2,1,0:T(8,128)S(1)}, f32[4,64,128]{2,1,0:T(8,128)}, u32[]{:S(2)}) copy-start(f32[4,64,128]{2,1,0:T(8,128)} %param.9) | copy-start | bytes 393220
  19.5 98.5 %all-reduce.2.cloned.1.call-start = ((), (), s32[]{:S(2)}) async-start(), calls=%async_computation.19 | async-start | bytes 262144 | tf_op jit(solution)/shard_map/psum | solution.py:31
  85.1 312.7 %reduce-scatter.10.cloned.1.call-start = ((), (), s32[]{:S(2)}) async-start(), calls=%async_computation.9 | async-start | bytes 73728 | tf_op jit(solution)/shard_map/reduce_scatter | solution.py:55
  118.0 97.2 %copy-start.1 = (f32[4,128,1024]{2,1,0:T(8,128)S(1)}, f32[4,128,1024]{2,1,0:T(8,128)}, u32[]{:S(2)}) copy-start(f32[4,128,1024]{2,1,0:T(8,128)} %param.10) | copy-start | bytes 6291460
  118.0 128.6 %copy-start.2 = (f32[3,128,1024]{2,1,0:T(8,128)S(1)}, f32[3,128,1024]{2,1,0:T(8,128)}, u32[]{:S(2)}) copy-start(f32[3,128,1024]{2,1,0:T(8,128)} %param.11) | copy-start | bytes 4718596
  344.0 110.2 %reduce-scatter.12.cloned.1.call-start = ((), (), s32[]{:S(2)}) async-start(), calls=%async_computation.10 | async-start | bytes 73728 | tf_op jit(solution)/shard_map/reduce_scatter | solution.py:51
  397.8 338.4 %copy-start.6 = (f32[16,128]{1,0:T(8,128)S(1)}, f32[16,128]{1,0:T(8,128)}, u32[]{:S(2)}) copy-start(f32[16,128]{1,0:T(8,128)} %reduce-scatter.10.cloned.1.call-done) | copy-start | bytes 24580
  399.9 110.5 %reduce-scatter.14.cloned.1.call-start = ((), (), s32[]{:S(2)}) async-start(), calls=%async_computation.11 | async-start | bytes 73728 | tf_op jit(solution)/shard_map/reduce_scatter | solution.py:55
  456.2 110.5 %reduce-scatter.16.cloned.1.call-start = ((), (), s32[]{:S(2)}) async-start(), calls=%async_computation.12 | async-start | bytes 73728 | tf_op jit(solution)/shard_map/reduce_scatter | solution.py:51
  510.4 225.8 %copy-start.7 = (f32[16,128]{1,0:T(8,128)S(1)}, f32[16,128]{1,0:T(8,128)}, u32[]{:S(2)}) copy-start(f32[16,128]{1,0:T(8,128)} %reduce-scatter.14.cloned.1.call-done) | copy-start | bytes 24580
  512.5 110.7 %reduce-scatter.18.cloned.1.call-start = ((), (), s32[]{:S(2)}) async-start(), calls=%async_computation.13 | async-start | bytes 73728 | tf_op jit(solution)/shard_map/reduce_scatter | solution.py:55
  568.8 110.8 %reduce-scatter.20.cloned.1.call-start = ((), (), s32[]{:S(2)}) async-start(), calls=%async_computation.14 | async-start | bytes 73728 | tf_op jit(solution)/shard_map/reduce_scatter | solution.py:51
  625.3 159.0 %copy-start.4 = (f32[128,512]{1,0:T(8,128)S(1)}, f32[128,512]{1,0:T(8,128)}, u32[]{:S(2)}) copy-start(f32[128,512]{1,0:T(8,128)} %param.8) | copy-start | bytes 786436
  625.3 110.9 %reduce-scatter.22.cloned.1.call-start = ((), (), s32[]{:S(2)}) async-start(), calls=%async_computation.15 | async-start | bytes 73728 | tf_op jit(solution)/shard_map/reduce_scatter | solution.py:55
  681.7 99.8 %all-gather.3.cloned.1.call-start = ((), (), s32[]{:S(2)}) async-start(), calls=%async_computation.16 | async-start | bytes 1179648 | tf_op jit(solution)/shard_map/all_gather | solution.py:57
  742.8 61.1 %copy-start.3 = (f32[4,64,128]{2,1,0:T(8,128)S(1)}, f32[4,64,128]{2,1,0:T(8,128)}, u32[]{:S(2)}) copy-start(f32[4,64,128]{2,1,0:T(8,128)} %all_gather.38) | copy-start | bytes 393220
  742.8 61.0 %reduce-scatter.24.cloned.1.call-start = ((), (), s32[]{:S(2)}) async-start(), calls=%async_computation.17 | async-start | bytes 163840 | tf_op jit(solution)/shard_map/reduce_scatter | solution.py:61
Sparse Core Ops, SparseCore 0:
  19.6 65.4 reduce-scatter.25
  87.5 30.4 all-reduce.1
  344.1 53.6 reduce-scatter.9
  401.4 52.7 reduce-scatter.11
  457.7 52.7 reduce-scatter.13
  514.0 52.7 reduce-scatter.15
  570.4 52.7 reduce-scatter.17
  626.9 52.7 reduce-scatter.19
  683.4 52.7 reduce-scatter.21
  742.9 38.5 all-gather.2
  785.4 18.4 reduce-scatter.23
where the time goes:
time: 812 us; the launch traced here: 811 us
  waiting for transfers between devices  535 us (66%)
  blocking collectives  229 us (28%)
  matrix products  29.9 us (4%)
  between operations  14 us (2%)
    reduce_scatter x4, waiting for transfers between devices, per_device(): lax.psum_scatter(solve_part, 'leaf', scatter_dimension=1, tiled=True)  217 us
    reduce_scatter x3, waiting for transfers between devices, per_device(): lax.psum_scatter(coupling_part, 'leaf', scatter_dimension=1, tiled=True)  163 us
    all_gather x4, blocking collectives, per_device(): known_full = lax.all_gather(known_part, 'leaf', axis=1, tiled=True)  123 us
    all_gather x3, blocking collectives, per_device(): y_full = lax.all_gather(y_level, 'leaf', axis=1, tiled=True)  92.3 us
    reduce_scatter x1, waiting for transfers between devices, per_device(): lax.psum_scatter(row_total, 'leaf', scatter_dimension=2, tiled=True)  65.5 us
    all_gather x1, waiting for transfers between devices, per_device(): solved_full = lax.all_gather(solved_stack, 'leaf', axis=2, tiled=True)  38.7 us
    psum x1, waiting for transfers between devices, per_device(): row_total = lax.psum(section_parts, 'row')  32.8 us
    reduce_scatter x1, waiting for transfers between devices, per_device(): lax.psum_scatter(section_part, 'row', scatter_dimension=1, tiled=True)  18.6 us
  transfers between devices with their start and end apart: 11, of which 11 were waited for; matrix products, arithmetic and copies ran while one was open for 0% of the time, Pallas kernels for 0%

commit v1 on v0

v1 whole, which is shorter than its diff:
```python
import functools

import jax
import jax.numpy as jnp
from jax import lax
from jax.experimental import pallas as pl
from jax.experimental.pallas import tpu as pltpu
from jax.sharding import PartitionSpec as P

MESH = pl.DeviceIdType.MESH
LAST = (((1,), (1,)), ((), ()))
PLAIN = (((1,), (0,)), ((), ()))
CHUNK = 8


def split(value):
    high = value.astype(jnp.bfloat16)
    low = (value - high.astype(jnp.float32)).astype(jnp.bfloat16)
    return high, low


def dot3(left, right, dims):
    rows = left.shape[0]
    high, low = split(left)
    both = jnp.concatenate([high, low], axis=0)
    first = lax.dot_general(both, right[0], dims, preferred_element_type=jnp.float32)
    second = lax.dot_general(high, right[1], dims, preferred_element_type=jnp.float32)
    return first[:rows] + (first[rows:] + second)


def lanes(ref, start, count):
    return jnp.concatenate([ref[start + i] for i in range(count)], axis=1)


def kernel(
    leaves, rows,
    rhs_h, dinv_h, srhs_h, sinv_h, coup_h, upd_h, link_ref,
    osec_h, osep_h,
    dinv, srhs, sinv, coup, upd,
    rhsb, parts, prow, rs_s, rs_r, fk, fy, bs_s, bs_r, xb, fin_s, fin_r, ob,
    in_sem, leaf_s, leaf_r, row_s, row_r, out_sem,
):
    leaf = lax.axis_index("leaf")
    row = lax.axis_index("row")
    levels = sinv.shape[0]
    q = srhs.shape[1]
    width = fk.shape[3]
    span = min(CHUNK, leaves)
    chunks = leaves // span

    def load(index, src, dst):
        copy = pltpu.make_async_copy(src, dst, in_sem.at[index])
        copy.start()
        return copy

    load_rhs = load(0, rhs_h, rhsb.at[row])
    load_dinv = load(1, dinv_h, dinv)
    load_upd = [load(2 + k, upd_h.at[k], upd.at[k]) for k in range(levels)]
    load_srhs = load(2 + levels, srhs_h.at[:, pl.ds(pl.multiple_of(row * q, q), q), :], srhs)
    load_sinv = load(3 + levels, sinv_h, sinv)
    load_coup = load(4 + levels, coup_h, coup)

    def each_leaf(body):
        def step(d, carry):
            body(lax.rem(leaf + d, leaves))
            return carry
        lax.fori_loop(1, leaves, step, 0)

    def each_row(body):
        for d in range(1, rows):
            body(lax.rem(row + d, rows))

    barrier = pltpu.get_barrier_semaphore()
    each_leaf(lambda p: pl.semaphore_signal(barrier, inc=1, device_id={"leaf": p}, device_id_type=MESH))
    each_row(lambda p: pl.semaphore_signal(barrier, inc=1, device_id={"row": p}, device_id_type=MESH))
    pl.semaphore_wait(barrier, leaves + rows - 2)

    def leaf_send(src_of, dst, index):
        each_leaf(lambda p: pltpu.make_async_remote_copy(
            src_ref=src_of(p), dst_ref=dst, send_sem=leaf_s.at[index], recv_sem=leaf_r.at[index],
            device_id={"leaf": p}, device_id_type=MESH).start())

    def row_send(src_of, dst, index):
        each_row(lambda p: pltpu.make_async_remote_copy(
            src_ref=src_of(p), dst_ref=dst, send_sem=row_s.at[index], recv_sem=row_r.at[index],
            device_id={"row": p}, device_id_type=MESH).start())

    def drain(buf, count, sem):
        ref = buf.at[pl.ds(0, count - 1)]
        pltpu.make_async_copy(ref, ref, sem).wait()

    red_i, fk_i, fy_i = 0, levels, 2 * levels
    bs_i, x_i = 3 * levels - 1, 5 * levels - 2
    part_i, gath_i, fin_i = 1, 1 + levels, 1 + 2 * levels

    row_send(lambda p: rhs_h, rhsb.at[row], 0)
    load_dinv.wait()
    dinv_split = split(dinv[...])
    load_rhs.wait()
    drain(rhsb, rows, row_r.at[0])
    rhs_full = jnp.concatenate([rhsb[i] for i in range(rows)], axis=1)
    y_sec = dot3(rhs_full, dinv_split, LAST)

    weights = [link_ref[0, k].astype(jnp.float32) for k in range(levels)]

    for k in range(levels):
        load_upd[k].wait()
        scaled = y_sec * weights[k]

        def part_step(c, k=k, scaled=scaled):
            cols = pl.ds(c * span * width, span * width)
            value = dot3(scaled, split(upd[k, cols, :]), LAST)
            parts[k, :, :, cols] = value.reshape(rows, q, span * width)

        if chunks == 1:
            part_step(0)
        else:
            pl.loop(0, chunks)(part_step)
        row_send(lambda p: parts.at[k, p], prow.at[k, row], part_i + k)

    def reduce_row(k):
        prow[k, row] = parts[k, row]
        drain(prow.at[k], rows, row_r.at[part_i + k])
        for i in range(leaves):
            cols = pl.ds(i * width, width)
            total = prow[k, 0, :, cols]
            for r in range(1, rows):
                total = total + prow[k, r, :, cols]
            rs_s[k, i] = total
        leaf_send(lambda p: rs_s.at[k, p], rs_r.at[k, leaf], red_i + k)
        rs_r[k, leaf] = rs_s[k, leaf]

    def add_up(ref):
        total = ref[0]
        for i in range(1, leaves):
            total = total + ref[i]
        return total

    def contract(buf, matrix, k, index):
        if chunks == 1:
            prepared = split(matrix[k])
            drain(buf, leaves, leaf_r.at[index])
            return dot3(lanes(buf, 0, span), prepared, LAST)
        drain(buf, leaves, leaf_r.at[index])

        def step(c, total):
            block = split(matrix[k, :, pl.ds(pl.multiple_of(c * span * width, span * width), span * width)])
            return total + dot3(lanes(buf, c * span, span), block, LAST)

        return lax.fori_loop(0, chunks, step, jnp.zeros((q, width), jnp.float32))

    def expand(value, matrix, prepared, k, slot):
        def store(c, block):
            product = dot3(value, block, PLAIN)
            for i in range(span):
                bs_s[slot, c * span + i] = product[:, i * width:(i + 1) * width]

        if chunks == 1:
            store(0, prepared)
        else:
            @pl.loop(0, chunks)
            def _(c):
                store(c, split(matrix[k, :, pl.ds(pl.multiple_of(c * span * width, span * width), span * width)]))
        leaf_send(lambda p: bs_s.at[slot, p], bs_r.at[slot, leaf], bs_i + slot)
        bs_r[slot, leaf] = bs_s[slot, leaf]

    def prepare(matrix, k):
        return split(matrix[k]) if chunks == 1 else None

    def collect(slot):
        drain(bs_r.at[slot], leaves, leaf_r.at[bs_i + slot])
        return add_up(bs_r.at[slot])

    reduce_row(0)
    load_srhs.wait()
    load_sinv.wait()
    load_coup.wait()
    y_leaf = []
    coupled = None
    for k in range(levels):
        drain(rs_r.at[k], leaves, leaf_r.at[red_i + k])
        known = srhs[k] - add_up(rs_r.at[k])
        if k > 0:
            known = known - coupled
        fk[k, leaf] = known
        leaf_send(lambda p: fk.at[k, leaf], fk.at[k, leaf], fk_i + k)
        if k < levels - 1:
            reduce_row(k + 1)
        y_level = contract(fk.at[k], sinv, k, fk_i + k)
        y_leaf.append(y_level)
        if k < levels - 1:
            fy[k, leaf] = y_level
            leaf_send(lambda p: fy.at[k, leaf], fy.at[k, leaf], fy_i + k)
            coupled = contract(fy.at[k], coup, k, fy_i + k)

    outs = []

    def pass_on(k):
        drain(xb.at[k, row], leaves, leaf_r.at[x_i + k])
        row_send(lambda p: xb.at[k, row], xb.at[k, row], gath_i + k)

    def back_term(k):
        def block_of(c):
            start = c * span * width
            if chunks > 1:
                start = pl.multiple_of(start, span * width)
            return split(upd[k, pl.ds(start, span * width), :])

        def gathered(c):
            return jnp.concatenate(
                [lanes(xb.at[k, r], c * span, span) for r in range(rows)], axis=0)

        prepared = block_of(0) if chunks == 1 else None
        drain(xb.at[k], rows, row_r.at[gath_i + k])
        copy = pltpu.make_async_copy(xb.at[k, :, leaf], osep_h.at[k], out_sem.at[k])
        copy.start()
        outs.append(copy)
        if chunks == 1:
            total = dot3(gathered(0), prepared, PLAIN)
        else:
            total = lax.fori_loop(
                0, chunks, lambda c, t: t + dot3(gathered(c), block_of(c), PLAIN),
                jnp.zeros((rows * q, width), jnp.float32))
        return total * weights[k]

    back = y_sec
    slot = 0
    adjusted = y_leaf[levels - 1]
    prepared = prepare(sinv, levels - 1)
    for k in range(levels - 1, -1, -1):
        expand(adjusted, sinv, prepared, k, slot)
        prepared = prepare(coup, k - 1) if k > 0 else None
        if k + 1 < levels:
            pass_on(k + 1)
        solved = collect(slot)
        slot += 1
        if k > 0:
            expand(solved, coup, prepared, k - 1, slot)
            xb[k, row, leaf] = solved
            leaf_send(lambda p: xb.at[k, row, leaf], xb.at[k, row, leaf], x_i + k)
            prepared = prepare(sinv, k - 1)
            if k + 1 < levels:
                back = back - back_term(k + 1)
            adjusted = y_leaf[k - 1] - collect(slot)
            slot += 1
        else:
            xb[k, row, leaf] = solved
            leaf_send(lambda p: xb.at[k, row, leaf], xb.at[k, row, leaf], x_i + k)
    back = back - back_term(1)
    pass_on(0)
    dinv_split = split(dinv[...])
    back = back - back_term(0)
    last = dot3(back, dinv_split, PLAIN)
    for r in range(rows):
        fin_s[r] = last[:, r * width:(r + 1) * width]
    row_send(lambda p: fin_s.at[p], fin_r.at[row], fin_i)
    fin_r[row] = fin_s[row]

    for k in range(levels):
        drain(rs_s.at[k], leaves, leaf_s.at[red_i + k])
        drain(fk.at[k], leaves, leaf_s.at[fk_i + k])
        drain(xb.at[k, row], leaves, leaf_s.at[x_i + k])
        drain(parts.at[k], rows, row_s.at[part_i + k])
        drain(xb.at[k], rows, row_s.at[gath_i + k])
        if k < levels - 1:
            drain(fy.at[k], leaves, leaf_s.at[fy_i + k])
    for s in range(2 * levels - 1):
        drain(bs_s.at[s], leaves, leaf_s.at[bs_i + s])
    drain(rhsb, rows, row_s.at[0])

    drain(fin_r, rows, row_r.at[fin_i])
    total = fin_r[0]
    for r in range(1, rows):
        total = total + fin_r[r]
    ob[...] = total
    copy = pltpu.make_async_copy(ob, osec_h, out_sem.at[levels])
    copy.start()
    outs.append(copy)
    drain(fin_s, rows, row_s.at[fin_i])
    for copy in outs:
        copy.wait()


def per_device(leaves, rows, sec_rhs, sec_inverse, sep_rhs, sep_inverse, sep_coupling, sec_update, link):
    levels, rhs, width = sep_rhs.shape
    full = sep_inverse.shape[2]
    q = rhs // rows
    f32 = jnp.float32
    any_spec = pl.BlockSpec(memory_space=pl.ANY)
    slots = lambda n: pltpu.VMEM((n, leaves, q, width), f32)
    vmem = lambda *shape: pltpu.VMEM(shape, f32)
    leaf_rounds = 6 * levels - 2
    row_rounds = 2 + 2 * levels
    scratch = [
        vmem(*sec_inverse.shape), vmem(levels, q, width), vmem(*sep_inverse.shape),
        vmem(*sep_coupling.shape), vmem(*sec_update.shape),
        vmem(rows, *sec_rhs.shape), vmem(levels, rows, q, full), vmem(levels, rows, q, full),
        slots(levels), slots(levels), slots(levels), slots(levels - 1),
        slots(2 * levels - 1), slots(2 * levels - 1),
        vmem(levels, rows, leaves, q, width),
        vmem(rows, *sec_rhs.shape), vmem(rows, *sec_rhs.shape), vmem(*sec_rhs.shape),
        pltpu.SemaphoreType.DMA((5 + levels,)),
        pltpu.SemaphoreType.DMA((leaf_rounds,)), pltpu.SemaphoreType.DMA((leaf_rounds,)),
        pltpu.SemaphoreType.DMA((row_rounds,)), pltpu.SemaphoreType.DMA((row_rounds,)),
        pltpu.SemaphoreType.DMA((levels + 1,)),
    ]
    sec, sep = pl.pallas_call(
        functools.partial(kernel, leaves, rows),
        out_shape=(
            jax.ShapeDtypeStruct(sec_rhs.shape, f32),
            jax.ShapeDtypeStruct((levels, rows, q, width), f32),
        ),
        in_specs=[any_spec] * 6 + [pl.BlockSpec(memory_space=pltpu.SMEM)],
        out_specs=(any_spec, any_spec),
        scratch_shapes=scratch,
        compiler_params=pltpu.CompilerParams(
            collective_id=0, has_side_effects=True, vmem_limit_bytes=58 * 1024 * 1024),
    )(sec_rhs, sec_inverse, sep_rhs, sep_inverse, sep_coupling, sec_update, link)
    return sec, sep.reshape(levels, rhs, width)


def solution(mesh):
    in_specs = (
        P(None, ("leaf", "row")),
        P(("leaf", "row"), None),
        P(None, None, "leaf"),
        P(None, "leaf", None),
        P(None, "leaf", None),
        P(None, None, ("leaf", "row")),
        P("leaf", None),
    )
    out_specs = (P(None, ("leaf", "row")), P(None, None, "leaf"))
    return jax.shard_map(
        functools.partial(per_device, mesh.shape["leaf"], mesh.shape["row"]),
        mesh=mesh, in_specs=in_specs, out_specs=out_specs, check_vma=False,
    )
```

time: 812 us -> 98.9 us (0.12)
  waiting for transfers between devices: 535 us -> 0 us
  blocking collectives: 229 us -> 0 us
  Pallas kernels: 0 us -> 95.1 us
  matrix products: 29.9 us -> 0 us
  between operations: 14 us -> 0.64 us
    reduce_scatter x9 -> x0, waiting for transfers between devices: 464 us -> none  [the longest x4 217 us: per_device(): lax.psum_scatter(solve_part, 'leaf', scatter_dimension=1, tiled=True)]
    all_gather x9 -> x0, blocking collectives: 229 us -> none  [the longest x4 123 us: per_device(): known_full = lax.all_gather(known_part, 'leaf', axis=1, tiled=True)]
    pallas_call x0 -> x1, Pallas kernels: none -> 95.1 us  [per_device(): pl.pallas_call(functools.partial(kernel, leaves, rows), out_shape=(jax.Sh...]
    all_gather x1 -> x0, waiting for transfers between devices: 38.7 us -> none  [per_device(): solved_full = lax.all_gather(solved_stack, 'leaf', axis=2, tiled=True)]
    psum x1 -> x0, waiting for transfers between devices: 32.8 us -> none  [per_device(): row_total = lax.psum(section_parts, 'row')]
    dot_general x18 -> x0, matrix products: 29.9 us -> none  [the longest x8 14.3 us: dot_plain(): jnp.dot(left, right, precision=lax.Precision.HIGHEST, preferred_element_t...]
  transfers between devices with their start and end apart: 11 -> 0, of which waited for: 11 -> 0; matrix products, arithmetic and copies ran while one was open for 0% -> 0% of each run, Pallas kernels for 0% -> 0%
where the time goes in v1:
time: 98.9 us; the launch traced here: 98.7 us
  Pallas kernels  95.1 us (96%)
  local copies, waits for them, and re-layouts  2.94 us (3%)
    pallas_call x1, Pallas kernels, per_device(): pl.pallas_call(functools.partial(kernel, leaves, rows), out_shape=(jax.Sh...  95.1 us
    unnamed x2, local copies, waits for them, and re-layouts  2.94 us

profile of v1, /device:TPU:0, one launch (start us, length us, event | category | flops | bytes accessed | tf_op | source)
XLA Modules:
  0.0 98.7 jit_solution(13164253016100776108)
XLA Ops:
  0.6 95.1 %shard_map.86 = (f32[64,128]{1,0:T(8,128)}, f32[4,4,16,128]{3,2,1,0:T(8,128)}) custom-call(f32[64,128]{1,0:T(8,128)} %rhs_h.1, f32[128,512]{1,0:T(8,128)} %dinv_h.1, f32[4,64,128]{2,1,0:T(8,128)} %srhs_h.1, f32[4,128,1024]{2,1,0:T(8,128)} %sinv_h.1, f32[3,128,1024]{2,1,0:T(8,128)} %coup_h.1, f32[4,1024,128]{2,1,0:T(8,128)} %upd_h.1, s32[1,4]{1,0:T(1,128)} %link_ref.1), custom_call_target="tpu_custom_call" | custom-call | tf_op jit(solution)/shard_map/pallas_call | solution.py:307
  95.8 1.4 %copy.11 = f32[64,128]{1,0:T(8,128)} copy(f32[64,128]{1,0:T(8,128)} %get-tuple-element.8) | data formatting | bytes 65536
  97.1 1.6 %copy.12 = f32[4,64,128]{2,1,0:T(8,128)} copy(f32[4,64,128]{2,1,0:T(8,128)} %bitcast.1) | data formatting | bytes 262144

commit v2 on v1

--- a/solution.py
+++ b/solution.py
@@ -37,7 +37,7 @@
     rhs_h, dinv_h, srhs_h, sinv_h, coup_h, upd_h, link_ref,
     osec_h, osep_h,
     dinv, srhs, sinv, coup, upd,
-    rhsb, parts, prow, rs_s, rs_r, fk, fy, bs_s, bs_r, xb, fin_s, fin_r, ob,
+    rhsb, parts, prow, rs_s, rs_r, fk, fy, bs_s, bs_r, xb, xs, u0, dfull, base_s, base_r, fin_s, fin_r,
     in_sem, leaf_s, leaf_r, row_s, row_r, out_sem,
 ):
     leaf = lax.axis_index("leaf")
@@ -92,6 +92,7 @@
     red_i, fk_i, fy_i = 0, levels, 2 * levels
     bs_i, x_i = 3 * levels - 1, 5 * levels - 2
     part_i, gath_i, fin_i = 1, 1 + levels, 1 + 2 * levels
+    base_i, u0_i, dfull_i = fin_i + 1, fin_i + 2, fin_i + 3
 
     row_send(lambda p: rhs_h, rhsb.at[row], 0)
     load_dinv.wait()
@@ -172,6 +173,10 @@
         return add_up(bs_r.at[slot])
 
     reduce_row(0)
+    row_send(lambda p: dinv_h, dfull.at[row], dfull_i)
+    row_send(lambda p: upd_h.at[0], u0.at[row], u0_i)
+    dfull[row] = dinv[...]
+    u0[row] = upd[0]
     load_srhs.wait()
     load_sinv.wait()
     load_coup.wait()
@@ -246,22 +251,51 @@
         else:
             xb[k, row, leaf] = solved
             leaf_send(lambda p: xb.at[k, row, leaf], xb.at[k, row, leaf], x_i + k)
+    row_send(lambda p: xb.at[0, row, leaf], xs.at[row], gath_i)
+    xs[row] = solved
     back = back - back_term(1)
-    pass_on(0)
-    dinv_split = split(dinv[...])
-    back = back - back_term(0)
-    last = dot3(back, dinv_split, PLAIN)
+    base_s[...] = back.reshape(rows, q, width)
+    row_send(lambda p: base_s.at[p], base_r.at[row], base_i)
+    base_r[row] = base_s[row]
+
+    drain(dfull, rows, row_r.at[dfull_i])
+    drain(u0, rows, row_r.at[u0_i])
+
+    def section_block(c):
+        start = c * span * width
+        if chunks > 1:
+            start = pl.multiple_of(start, span * width)
+        return split(jnp.concatenate(
+            [u0[r, pl.ds(start, span * width), :] for r in range(rows)], axis=1))
+
+    prepared = section_block(0) if chunks == 1 else None
+    dinv_split = split(jnp.concatenate([dfull[r] for r in range(rows)], axis=0))
+    drain(xb.at[0, row], leaves, leaf_r.at[x_i])
+    if chunks == 1:
+        term = dot3(lanes(xb.at[0, row], 0, span), prepared, PLAIN)
+    else:
+        term = lax.fori_loop(
+            0, chunks,
+            lambda c, t: t + dot3(lanes(xb.at[0, row], c * span, span), section_block(c), PLAIN),
+            jnp.zeros((q, rows * width), jnp.float32))
+    drain(base_r, rows, row_r.at[base_i])
+    base = jnp.concatenate([base_r[r] for r in range(rows)], axis=1)
+    last = dot3(base - term * weights[0], dinv_split, PLAIN)
     for r in range(rows):
         fin_s[r] = last[:, r * width:(r + 1) * width]
     row_send(lambda p: fin_s.at[p], fin_r.at[row], fin_i)
     fin_r[row] = fin_s[row]
+    drain(xs, rows, row_r.at[gath_i])
+    copy = pltpu.make_async_copy(xs, osep_h.at[0], out_sem.at[0])
+    copy.start()
+    outs.append(copy)
 
     for k in range(levels):
         drain(rs_s.at[k], leaves, leaf_s.at[red_i + k])
         drain(fk.at[k], leaves, leaf_s.at[fk_i + k])
         drain(xb.at[k, row], leaves, leaf_s.at[x_i + k])
         drain(parts.at[k], rows, row_s.at[part_i + k])
-        drain(xb.at[k], rows, row_s.at[gath_i + k])
+        drain(xb.at[k] if k > 0 else xs, rows, row_s.at[gath_i + k])
         if k < levels - 1:
             drain(fy.at[k], leaves, leaf_s.at[fy_i + k])
     for s in range(2 * levels - 1):
@@ -269,13 +303,12 @@
     drain(rhsb, rows, row_s.at[0])
 
     drain(fin_r, rows, row_r.at[fin_i])
-    total = fin_r[0]
-    for r in range(1, rows):
-        total = total + fin_r[r]
-    ob[...] = total
-    copy = pltpu.make_async_copy(ob, osec_h, out_sem.at[levels])
+    copy = pltpu.make_async_copy(fin_r, osec_h, out_sem.at[levels])
     copy.start()
     outs.append(copy)
+    drain(base_s, rows, row_s.at[base_i])
+    drain(dfull, rows, row_s.at[dfull_i])
+    drain(u0, rows, row_s.at[u0_i])
     drain(fin_s, rows, row_s.at[fin_i])
     for copy in outs:
         copy.wait()
@@ -290,7 +323,7 @@
     slots = lambda n: pltpu.VMEM((n, leaves, q, width), f32)
     vmem = lambda *shape: pltpu.VMEM(shape, f32)
     leaf_rounds = 6 * levels - 2
-    row_rounds = 2 + 2 * levels
+    row_rounds = 5 + 2 * levels
     scratch = [
         vmem(*sec_inverse.shape), vmem(levels, q, width), vmem(*sep_inverse.shape),
         vmem(*sep_coupling.shape), vmem(*sec_update.shape),
@@ -298,7 +331,8 @@
         slots(levels), slots(levels), slots(levels), slots(levels - 1),
         slots(2 * levels - 1), slots(2 * levels - 1),
         vmem(levels, rows, leaves, q, width),
-        vmem(rows, *sec_rhs.shape), vmem(rows, *sec_rhs.shape), vmem(*sec_rhs.shape),
+        vmem(rows, q, width), vmem(rows, full, width), vmem(rows, *sec_inverse.shape),
+        vmem(rows, q, width), vmem(rows, q, width), vmem(rows, q, width), vmem(rows, q, width),
         pltpu.SemaphoreType.DMA((5 + levels,)),
         pltpu.SemaphoreType.DMA((leaf_rounds,)), pltpu.SemaphoreType.DMA((leaf_rounds,)),
         pltpu.SemaphoreType.DMA((row_rounds,)), pltpu.SemaphoreType.DMA((row_rounds,)),
@@ -307,7 +341,7 @@
     sec, sep = pl.pallas_call(
         functools.partial(kernel, leaves, rows),
         out_shape=(
-            jax.ShapeDtypeStruct(sec_rhs.shape, f32),
+            jax.ShapeDtypeStruct((rows, q, width), f32),
             jax.ShapeDtypeStruct((levels, rows, q, width), f32),
         ),
         in_specs=[any_spec] * 6 + [pl.BlockSpec(memory_space=pltpu.SMEM)],
@@ -316,7 +350,7 @@
         compiler_params=pltpu.CompilerParams(
             collective_id=0, has_side_effects=True, vmem_limit_bytes=58 * 1024 * 1024),
     )(sec_rhs, sec_inverse, sep_rhs, sep_inverse, sep_coupling, sec_update, link)
-    return sec, sep.reshape(levels, rhs, width)
+    return sec.reshape(rhs, width), sep.reshape(levels, rhs, width)
 
 
 def solution(mesh):

time: 98.9 us -> 95.5 us (0.966)
  Pallas kernels: 95.1 us -> 91.7 us
    pallas_call x1, Pallas kernels: 95.1 us -> 91.7 us  [per_device(): pl.pallas_call(functools.partial(kernel, leaves, rows), out_shape=(jax.Sh...]
where the time goes in v2:
time: 95.5 us; the launch traced here: 95.3 us
  Pallas kernels  91.7 us (96%)
  local copies, waits for them, and re-layouts  2.94 us (3%)
    pallas_call x1, Pallas kernels, per_device(): pl.pallas_call(functools.partial(kernel, leaves, rows), out_shape=(jax.Sh...  91.7 us
    unnamed x2, local copies, waits for them, and re-layouts  2.94 us

profile of v2, /device:TPU:0, one launch (start us, length us, event | category | flops | bytes accessed | tf_op | source)
XLA Modules:
  0.0 95.3 jit_solution(16650796100782247932)
XLA Ops:
  0.6 91.7 %shard_map.86 = (f32[4,16,128]{2,1,0:T(8,128)}, f32[4,4,16,128]{3,2,1,0:T(8,128)}) custom-call(f32[64,128]{1,0:T(8,128)} %rhs_h.1, f32[128,512]{1,0:T(8,128)} %dinv_h.1, f32[4,64,128]{2,1,0:T(8,128)} %srhs_h.1, f32[4,128,1024]{2,1,0:T(8,128)} %sinv_h.1, f32[3,128,1024]{2,1,0:T(8,128)} %coup_h.1, f32[4,1024,128]{2,1,0:T(8,128)} %upd_h.1, s32[1,4]{1,0:T(1,128)} %link_ref.1), custom_call_target="tpu_custom_call" | custom-call | tf_op jit(solution)/shard_map/pallas_call | solution.py:341
  92.3 1.4 %copy.11 = f32[64,128]{1,0:T(8,128)} copy(f32[64,128]{1,0:T(8,128)} %bitcast.3) | data formatting | bytes 65536
  93.7 1.6 %copy.12 = f32[4,64,128]{2,1,0:T(8,128)} copy(f32[4,64,128]{2,1,0:T(8,128)} %bitcast.2) | data formatting | bytes 262144
